TPU v7x, 128 devices: a whole 4x4x4 slice. The times are simulated.
128 devices in a mesh: ctx: 32 (over z, x, core), head: 4 (over y).
Axes of the slice: x: 4, y: 4, z: 4, core: 2. Of those that a mesh axis runs over, the one named last changes fastest.
Arguments:
- tokens: bfloat16 [8192, 3072], P('ctx', 'head'), may hold values from -6 to 6
- query_key_value_weight: bfloat16 [3, 3072, 4096], P(None, None, 'head'), may hold values from -0.109375 to 0.109375
- output_weight: bfloat16 [4096, 3072], P('head'), may hold values from -0.09375 to 0.09375
- input_down_weights: bfloat16 [3, 3072, 16], P(None, 'head'), may hold values from -0.109375 to 0.109375
- input_up_weights: bfloat16 [3, 16, 4096], P(None, None, 'head'), may hold values from -1.5 to 1.5
- output_down_weight: bfloat16 [4096, 16], P('head'), may hold values from -0.09375 to 0.09375
- output_up_weight: bfloat16 [16, 3072], P(None, 'head'), may hold values from -1.5 to 1.5
- cotangent: bfloat16 [8192, 3072], P('ctx', 'head'), may hold values from -6 to 6
Outputs:
- output: bfloat16 [8192, 3072], P('ctx', 'head')
- input_grad: bfloat16 [8192, 3072], P('ctx', 'head')
- grad_down_qkv: float32 [3, 3072, 16], P(None, 'head')
- grad_up_qkv: float32 [3, 16, 4096], P(None, None, 'head')
- grad_down_out: float32 [4096, 16], P('head')
- grad_up_out: float32 [16, 3072], P(None, 'head')
All inputs are finite; a program needn't handle non-finite values.
Results may differ from a plain program's by a relative error of at most 0.029.
Values may be sent and summed in bfloat16 or wider, within the bound.
No kernel may reach another device: no remote copies, remote signals or barrier semaphores. Data moves between devices by JAX's collectives and lax.ppermute only.
A program may use at most 128 MiB of HBM per device.

v0:
```python
import jax
import jax.numpy as jnp
from jax import lax
from jax.sharding import PartitionSpec as P

HEAD_DIM = 128
BLOCK = 256


adapter_scale = 0.5
epsilon = 1e-06


def entering(array, axis, combine, identity, reverse):
    length, mine = (lax.axis_size(axis), lax.axis_index(axis))
    everything = lax.all_gather(array.astype(jnp.bfloat16), axis)
    start = jnp.broadcast_to(jnp.asarray(identity, array.dtype), array.shape)

    def hop(k, before):
        at = length - 1 - k if reverse else k
        reached = at > mine if reverse else at < mine
        new = combine(before, everything[at].astype(array.dtype))
        return jnp.where(reached, new, before)

    return lax.fori_loop(0, length, hop, start)


def causal_mask(length):
    position = jnp.arange(length)
    return position[:, None] >= position[None, :]


def add_states(earlier, later):
    return earlier + later


def forward_block(kv_state, blocks):
    q_block, k_block, v_block = blocks
    lower_mask = causal_mask(q_block.shape[0])
    scores = jnp.einsum("sjd,tjd->jst", q_block, k_block, preferred_element_type=jnp.float32)
    scores = jnp.where(lower_mask[None], scores, 0.0).astype(jnp.bfloat16)
    held_state = kv_state.astype(jnp.bfloat16)
    raw_out = jnp.einsum("jst,tje->sje", scores, v_block, preferred_element_type=jnp.float32)
    raw_out = raw_out + jnp.einsum(
        "sjd,jde->sje", q_block, held_state, preferred_element_type=jnp.float32
    )
    kv_state = kv_state + jnp.einsum(
        "tjd,tje->jde", k_block, v_block, preferred_element_type=jnp.float32
    )
    return (kv_state, (raw_out, held_state))


def backward_block(suffix_state, blocks):
    q_block, k_block, v_block, d_block, held_state = blocks
    lower_mask = causal_mask(q_block.shape[0])
    scores = jnp.einsum("sjd,tjd->jst", q_block, k_block, preferred_element_type=jnp.float32)
    scores = jnp.where(lower_mask[None], scores, 0.0).astype(jnp.bfloat16)
    d_scores = jnp.einsum("sje,tje->jst", d_block, v_block, preferred_element_type=jnp.float32)
    d_scores = jnp.where(lower_mask[None], d_scores, 0.0).astype(jnp.bfloat16)
    held_suffix = suffix_state.astype(jnp.bfloat16)
    d_query = jnp.einsum("jst,tjd->sjd", d_scores, k_block, preferred_element_type=jnp.float32)
    d_query = d_query + jnp.einsum(
        "sje,jde->sjd", d_block, held_state, preferred_element_type=jnp.float32
    )
    d_key = jnp.einsum("jst,sjd->tjd", d_scores, q_block, preferred_element_type=jnp.float32)
    d_key = d_key + jnp.einsum(
        "tje,jde->tjd", v_block, held_suffix, preferred_element_type=jnp.float32
    )
    d_value = jnp.einsum("jst,sje->tje", scores, d_block, preferred_element_type=jnp.float32)
    d_value = d_value + jnp.einsum(
        "tjd,jde->tje", k_block, held_suffix, preferred_element_type=jnp.float32
    )
    suffix_state = suffix_state + jnp.einsum(
        "sjd,sje->jde", q_block, d_block, preferred_element_type=jnp.float32
    )
    return (
        suffix_state,
        (d_query.astype(jnp.bfloat16), d_key.astype(jnp.bfloat16), d_value.astype(jnp.bfloat16)),
    )


def on_device(
    tokens,
    query_key_value_weight,
    output_weight,
    input_down_weights,
    input_up_weights,
    output_down_weight,
    output_up_weight,
    cotangent,
):
    count_of_rows = tokens.shape[0]
    local_cols = query_key_value_weight.shape[2]
    head_local = local_cols // HEAD_DIM
    block_count = count_of_rows // BLOCK
    scale_factor = adapter_scale * (count_of_rows * lax.axis_size("ctx")) ** (-0.5)
    segment = lax.all_gather(tokens, "head", axis=1, tiled=True)
    d_rows = lax.all_gather(input_down_weights, "head", axis=1, tiled=True)
    proj_sum = jnp.einsum(
        "tc,icn->itn", segment, query_key_value_weight, preferred_element_type=jnp.float32
    )
    low_sum = jnp.einsum("tc,icr->itr", segment, d_rows, preferred_element_type=jnp.float32)
    proj_sum, low_sum = (proj_sum, low_sum)
    low_rank_rows = low_sum.astype(jnp.bfloat16)
    projected_rows = (
        proj_sum
        + adapter_scale
        * jnp.einsum(
            "itr,irn->itn", low_rank_rows, input_up_weights, preferred_element_type=jnp.float32
        )
    ).astype(jnp.bfloat16)
    per_head = projected_rows.reshape(3, count_of_rows, head_local, HEAD_DIM)
    blocked = projected_rows.reshape(3, block_count, BLOCK, head_local, HEAD_DIM)
    local_total = jnp.einsum(
        "tjd,tje->jde", per_head[1], per_head[2], preferred_element_type=jnp.float32
    )
    prefix = entering(local_total, "ctx", add_states, jnp.zeros_like(local_total), False)
    final_state, (raw_out, held_state) = lax.scan(
        forward_block, prefix, (blocked[0], blocked[1], blocked[2])
    )
    raw_out = raw_out.reshape(count_of_rows, head_local, HEAD_DIM)
    root_mean = jnp.sqrt(jnp.mean(raw_out * raw_out, axis=-1, keepdims=True) + epsilon)
    normed = raw_out / root_mean
    attended_output = normed.astype(jnp.bfloat16).reshape(count_of_rows, local_cols)
    mid_sum = lax.psum(
        jnp.dot(attended_output, output_down_weight, preferred_element_type=jnp.float32), "head"
    )
    middle_rank_rows = mid_sum.astype(jnp.bfloat16)
    output_portion = lax.psum_scatter(
        jnp.dot(attended_output, output_weight, preferred_element_type=jnp.float32).astype(
            jnp.bfloat16
        ),
        "head",
        scatter_dimension=1,
        tiled=True,
    ).astype(jnp.float32)
    output = (
        output_portion
        + adapter_scale
        * jnp.dot(middle_rank_rows, output_up_weight, preferred_element_type=jnp.float32)
    ).astype(jnp.bfloat16)
    gradient_accumulator = jnp.einsum(
        "tc,nc->tn",
        lax.all_gather(cotangent, "head", axis=1, tiled=True),
        output_weight,
        preferred_element_type=jnp.float32,
    )
    back_sum = lax.psum(
        jnp.dot(cotangent, output_up_weight.T, preferred_element_type=jnp.float32), "head"
    )
    backward_middle = back_sum.astype(jnp.bfloat16)
    attended_gradient = gradient_accumulator + adapter_scale * jnp.dot(
        backward_middle, output_down_weight.T, preferred_element_type=jnp.float32
    )
    attended_gradient = attended_gradient.reshape(count_of_rows, head_local, HEAD_DIM)
    d_raw = (
        (attended_gradient - normed * jnp.mean(attended_gradient * normed, axis=-1, keepdims=True))
        / root_mean
    ).astype(jnp.bfloat16)
    suffix_total = jnp.einsum(
        "tjd,tje->jde", per_head[0], d_raw, preferred_element_type=jnp.float32
    )
    suffix = entering(suffix_total, "ctx", add_states, jnp.zeros_like(suffix_total), True)
    d_blocks = d_raw.reshape(block_count, BLOCK, head_local, HEAD_DIM)
    last_state, grad_parts = lax.scan(
        backward_block,
        suffix,
        (blocked[0], blocked[1], blocked[2], d_blocks, held_state),
        reverse=True,
    )
    d_proj = jnp.stack(grad_parts).reshape(3, count_of_rows, local_cols)
    low_part = jnp.einsum(
        "itn,irn->itr", d_proj, input_up_weights, preferred_element_type=jnp.float32
    )
    backward_low_rank = lax.psum(low_part.astype(jnp.bfloat16), "head")
    grad_part = jnp.einsum(
        "itn,icn->tc", d_proj, query_key_value_weight, preferred_element_type=jnp.float32
    )
    grad_sum = lax.psum_scatter(
        grad_part.astype(jnp.bfloat16), "head", scatter_dimension=1, tiled=True
    ).astype(jnp.float32)
    input_grad = (
        grad_sum
        + adapter_scale
        * jnp.einsum(
            "itr,icr->tc", backward_low_rank, input_down_weights, preferred_element_type=jnp.float32
        )
    ).astype(jnp.bfloat16)
    part_down_qkv = jnp.einsum(
        "tc,itr->icr", tokens, backward_low_rank, preferred_element_type=jnp.float32
    )
    part_up_qkv = jnp.einsum(
        "itr,itn->irn", low_rank_rows, d_proj, preferred_element_type=jnp.float32
    )
    part_down_out = jnp.dot(attended_output.T, backward_middle, preferred_element_type=jnp.float32)
    part_up_out = jnp.dot(middle_rank_rows.T, cotangent, preferred_element_type=jnp.float32)
    sum_down_qkv, sum_up_qkv, sum_down_out, sum_up_out = (
        lax.psum(part_down_qkv.astype(jnp.bfloat16), "ctx").astype(jnp.float32),
        lax.psum(part_up_qkv.astype(jnp.bfloat16), "ctx").astype(jnp.float32),
        lax.psum(part_down_out.astype(jnp.bfloat16), "ctx").astype(jnp.float32),
        lax.psum(part_up_out.astype(jnp.bfloat16), "ctx").astype(jnp.float32),
    )
    return (
        output,
        input_grad,
        scale_factor * sum_down_qkv,
        scale_factor * sum_up_qkv,
        scale_factor * sum_down_out,
        scale_factor * sum_up_out,
    )


def solution(mesh):
    return jax.shard_map(
        on_device,
        mesh=mesh,
        in_specs=(
            P("ctx", "head"),
            P(None, None, "head"),
            P("head", None),
            P(None, "head", None),
            P(None, None, "head"),
            P("head", None),
            P(None, "head"),
            P("ctx", "head"),
        ),
        out_specs=(
            P("ctx", "head"),
            P("ctx", "head"),
            P(None, "head", None),
            P(None, None, "head"),
            P("head", None),
            P(None, "head"),
        ),
        check_vma=False,
    )
```

profile of v0, /device:TPU:1, one launch (start us, length us, event | category | flops | bytes accessed | tf_op | source)
XLA Modules:
  0.0 454.2 jit_solution(10576288936163144294)
XLA Ops:
  8.7 11.8 %all_gather.22 = bf16[3,3072,16]{1,2,0:T(8,128)(2,1)S(1)} all-gather(bf16[3,768,16]{1,2,0:T(8,128)(2,1)} %param.15), channel_id=1, replica_groups=mesh['ctx'=32,'head'=4] {'head'}, dimensions={1}, use_global_device_ids=true | all-gather | bytes 368640 | tf_op jit(solution)/shard_map/all_gather | solution.py:98
  20.5 19.0 %all-gather.7.cloned.1.call-done = bf16[256,3072]{1,0:T(8,128)(2,1)} async-done(((bf16[256,768]{1,0:T(8,128)(2,1)}), bf16[256,3072]{1,0:T(8,128)(2,1)}) %all-gather.7.cloned.1.call-update) | async-done | bytes 1572880 | tf_op jit(solution)/shard_map/all_gather | solution.py:97
  39.5 2.1 fusion.17
  41.6 9.1 %fusion.4 = f32[3,1024,256]{2,1,0:T(8,128)S(1)} fusion(bf16[3,3072,1024]{2,1,0:T(8,128)(2,1)} %param.13, bf16[256,3072]{1,0:T(8,128)(2,1)S(1)} %copy-done.14), kind=kOutput, calls=%fused_computation.12 | convolution fusion | flops 4831838208 | bytes 23592960 | tf_op jit(solution)/shard_map/tc,icn->itn/dot_general | solution.py:99
  53.4 1.5 fusion.31
  54.9 12.8 %all-gather.9.cloned.1.call-done = bf16[256,3072]{1,0:T(8,128)(2,1)} async-done(((bf16[256,768]{1,0:T(8,128)(2,1)}), bf16[256,3072]{1,0:T(8,128)(2,1)}) %all-gather.9.cloned.1.call-update) | async-done | bytes 1572880 | tf_op jit(solution)/shard_map/all_gather | solution.py:144
  67.7 6.1 %fusion.32 = f32[256,1024]{1,0:T(8,128)} fusion(bf16[256,3072]{1,0:T(8,128)(2,1)} %all-gather.9.cloned.1.call-done, bf16[1024,3072]{1,0:T(8,128)(2,1)} %param.14), kind=kOutput, calls=%fused_computation.63 | convolution fusion | flops 1610612736 | bytes 8912896 | tf_op jit(solution)/shard_map/tc,nc->tn/dot_general | solution.py:142
  73.8 50.3 %all-gather.11.cloned.1.call-done = bf16[256,128,128]{2,1,0:T(8,128)(2,1)} async-done(((bf16[8,128,128]{2,1,0:T(8,128)(2,1)}), bf16[256,128,128]{2,1,0:T(8,128)(2,1)}) %all-gather.11.cloned.1.call-update) | async-done | bytes 8388624 | tf_op jit(solution)/shard_map/all_gather | solution.py:16
  124.1 40.2 %while.20 = (s32[]{:T(128)}, f32[8,128,128]{2,1,0:T(8,128)S(1)}, s32[]{:T(128)}, bf16[32,8,128,128]{3,2,1,0:T(8,128)(2,1)}, s32[]{:T(128)}, /*index=5*/s32[]{:T(128)}) while((s32[]{:T(128)}, f32[8,128,128]{2,1,0:T(8,128)S(1)}, s32[]{:T(128)}, bf16[32,8,128,128]{3,2,1,0:T(8,128)(2,1)}, s32[]{:T(128)}, /*index=5*/s32[]{:T(128)}) %tuple.100), condition=%wide.region_1.2_spmd.clone, body=%wide.region_0.1_spmd.clone.sunk | while | flops 524292 | bytes 1310821 | solution.py:25
  125.4 1.2 add_select_fusion.4
  126.6 1.2 add_select_fusion.4
  127.9 1.2 add_select_fusion.4
  129.2 1.2 add_select_fusion.4
  130.4 1.2 add_select_fusion.4
  132.9 1.2 add_select_fusion.4
  134.2 1.2 add_select_fusion.4
  135.4 1.2 add_select_fusion.4
  136.7 1.2 add_select_fusion.4
  138.0 1.2 add_select_fusion.4
  164.4 1.6 multiply_reduce_fusion.1
  167.1 13.3 %all-reduce = (bf16[256,16]{0,1:T(8,128)(2,1)S(1)}, bf16[256,16]{0,1:T(8,128)(2,1)S(1)}) all-reduce(f32[256,16]{0,1:T(8,128)S(1)} %fusion.37, f32[256,16]{0,1:T(8,128)S(1)} %fusion.33), channel_id=1, replica_groups=mesh['ctx'=32,'head'=4] {'head'}, use_global_device_ids=true, to_apply=%region_4.5 | all-reduce | flops 8192 | bytes 49152 | tf_op jit(solution)/shard_map/psum | solution.py:125
  180.4 2.5 fusion.6
  182.9 2.6 copy.39
  185.4 1.5 multiply_reduce_fusion
  191.8 2.6 fusion.36
  194.5 1.3 fusion.35
  195.8 5.8 %convolution_convert_fusion = bf16[256,3072]{1,0:T(8,128)(2,1)} fusion(bf16[256,1024]{0,1:T(8,128)(2,1)S(1)} %bitcast.117, bf16[1024,3072]{1,0:T(8,128)(2,1)} %param.14), kind=kOutput, calls=%fused_computation.3 | convolution fusion | flops 1611399168 | bytes 8388608 | tf_op jit(solution)/shard_map/dot_general | solution.py:130
  201.6 42.3 %all-gather.13.cloned.1.call-done = bf16[256,128,128]{2,1,0:T(8,128)(2,1)} async-done(((bf16[8,128,128]{2,1,0:T(8,128)(2,1)}), bf16[256,128,128]{2,1,0:T(8,128)(2,1)}) %all-gather.13.cloned.1.call-update) | async-done | bytes 8388624 | tf_op jit(solution)/shard_map/all_gather | solution.py:16
  243.9 40.4 %while.21 = (s32[]{:T(128)}, f32[8,128,128]{2,1,0:T(8,128)S(1)}, s32[]{:T(128)}, bf16[32,8,128,128]{3,2,1,0:T(8,128)(2,1)}, s32[]{:T(128)}, /*index=5*/s32[]{:T(128)}, s32[]{:T(128)}, s32[]{:T(128)}) while((s32[]{:T(128)}, f32[8,128,128]{2,1,0:T(8,128)S(1)}, s32[]{:T(128)}, bf16[32,8,128,128]{3,2,1,0:T(8,128)(2,1)}, s32[]{:T(128)}, ...), condition=%wide.region_8.9_spmd.clone, body=%wide.region_7.8_spmd.clone.sunk | while | flops 524296 | bytes 1310883 | solution.py:25
  254.0 1.2 add_select_fusion.5
  259.0 1.2 add_select_fusion.5
  260.3 1.2 add_select_fusion.5
  261.6 1.2 add_select_fusion.5
  262.8 1.2 add_select_fusion.5
  264.1 1.2 add_select_fusion.5
  265.4 1.2 add_select_fusion.5
  266.6 1.2 add_select_fusion.5
  267.9 1.2 add_select_fusion.5
  269.2 1.2 add_select_fusion.5
  284.3 1.6 fusion.11
  287.8 1.8 convolution_convert_fusion.6
  289.6 13.3 %psum.51 = bf16[3,256,16]{1,2,0:T(8,128)(2,1)S(1)} all-reduce(bf16[3,256,16]{1,2,0:T(8,128)(2,1)S(1)} %convolution_convert_fusion.6), channel_id=1, replica_groups=mesh['ctx'=32,'head'=4] {'head'}, use_global_device_ids=true, to_apply=%region_10.11 | all-reduce | flops 12288 | bytes 49152 | tf_op jit(solution)/shard_map/psum | solution.py:175
  304.9 10.4 %fusion = bf16[256,3072]{1,0:T(8,128)(2,1)} fusion(bf16[3,3072,1024]{2,1,0:T(8,128)(2,1)} %param.13, bf16[1,256,1024]{2,1,0:T(8,128)(2,1)S(1)} %copy-done.16, bf16[1,256,1024]{2,1,0:T(8,128)(2,1)S(1)} %copy.48, bf16[1,256,1024]{2,1,0:T(8,128)(2,1)S(1)} %copy-done.15), kind=kOutput, calls=%fused_computation.4 | convolution fusion | flops 4834197504 | bytes 22020096 | tf_op jit(solution)/shard_map/itn,icn->tc/dot_general | solution.py:176
  316.6 122.3 %all-reduce.1 = (bf16[1024,16]{0,1:T(8,128)(2,1)S(1)}, bf16[16,768]{1,0:T(8,128)(2,1)S(1)}) all-reduce(bf16[1024,16]{0,1:T(8,128)(2,1)S(1)} %convolution_convert_fusion.5, bf16[16,768]{1,0:T(8,128)(2,1)S(1)} %convolution_convert_fusion.7), channel_id=1, replica_groups=mesh['ctx'=32,'head'=4] {'ctx'}, use_global_device_ids=true, to_apply=%region_13.14 | all-reduce | flops 28672 | bytes 114688 | tf_op jit(solution)/shard_map/psum | solution.py:200
  440.2 2.0 fusion.15
  442.2 1.6 convert_multiply_fusion.1
  443.8 1.6 convert_multiply_fusion
  445.4 2.0 fusion.14
  (128 shorter events, 70.9 us)
Async XLA Ops:
  7.2 43.5 %copy-start = (bf16[3,16,1024]{2,1,0:T(8,128)(2,1)S(1)}, bf16[3,16,1024]{2,1,0:T(8,128)(2,1)}, u32[]{:S(2)}) copy-start(bf16[3,16,1024]{2,1,0:T(8,128)(2,1)} %param.16) | copy-start | bytes 294916
  7.2 32.3 %all-gather.7.cloned.1.call-start = ((), (), s32[]{:S(2)}) async-start(), calls=%async_computation.2 | async-start | bytes 1966080 | tf_op jit(solution)/shard_map/all_gather | solution.py:97
  7.9 59.8 %all-gather.9.cloned.1.call-start = ((), (), s32[]{:S(2)}) async-start(), calls=%async_computation.4 | async-start | bytes 1966080 | tf_op jit(solution)/shard_map/all_gather | solution.py:144
  8.7 115.5 %all-gather.11.cloned.1.call-start = ((), (), s32[]{:S(2)}) async-start(), calls=%async_computation.6 | async-start | bytes 8650752 | tf_op jit(solution)/shard_map/all_gather | solution.py:16
  39.5 2.1 copy-start.14
  51.4 112.9 %copy-start.1 = (bf16[1,256,1024]{1,2,0:T(8,128)(2,1)}, bf16[1,256,1024]{1,2,0:T(8,128)(2,1)S(1)}, u32[]{:S(2)}) copy-start(bf16[1,256,1024]{1,2,0:T(8,128)(2,1)S(1)} %get-tuple-element.301) | copy-start | bytes 1572868
  51.4 1.2 copy-start.11
  51.4 1.2 copy-start.18
  52.5 191.4 %all-gather.13.cloned.1.call-start = ((), (), s32[]{:S(2)}) async-start(), calls=%async_computation.7 | async-start | bytes 8650752 | tf_op jit(solution)/shard_map/all_gather | solution.py:16
  53.4 20.4 %copy-start.6 = (bf16[8,256,256]{2,1,0:T(8,128)(2,1)}, bf16[8,256,256]{2,1,0:T(8,128)(2,1)S(1)}, u32[]{:S(2)}) copy-start(bf16[8,256,256]{2,1,0:T(8,128)(2,1)S(1)} %select_convert_fusion.1) | copy-start | bytes 3145732
  165.9 0.9 copy-start.17
  166.1 0.8 copy-start.4
  185.4 1.5 copy-start.9
  186.9 1.1 copy-start.2
  189.0 251.2 %reduce-scatter.3.cloned.1.call-start = ((), (), s32[]{:S(2)}) async-start(), calls=%async_computation.3 | async-start | bytes 1966080 | tf_op jit(solution)/shard_map/reduce_scatter | solution.py:129
  189.7 1.1 copy-start.7
  191.8 2.6 copy-start.3
  191.8 2.6 copy-start.8
  194.5 1.3 copy-start.5
  201.6 240.7 %all-reduce.5.cloned.1.call-start = ((), (), s32[]{:S(2)}) async-start(), calls=%async_computation.8 | async-start | bytes 344064 | tf_op jit(solution)/shard_map/psum | solution.py:198
  285.9 1.4 copy-start.10
  287.8 15.1 %copy-start.15 = (bf16[1,256,1024]{2,1,0:T(8,128)(2,1)S(1)}, bf16[1,256,1024]{2,1,0:T(8,128)(2,1)}, u32[]{:S(2)}) copy-start(bf16[1,256,1024]{2,1,0:T(8,128)(2,1)} %copy.47) | copy-start | bytes 1572868
  287.8 15.1 %copy-start.16 = (bf16[1,256,1024]{2,1,0:T(8,128)(2,1)S(1)}, bf16[1,256,1024]{2,1,0:T(8,128)(2,1)}, u32[]{:S(2)}) copy-start(bf16[1,256,1024]{2,1,0:T(8,128)(2,1)} %copy.49) | copy-start | bytes 1572868
  302.9 1.0 copy-start.13
  304.8 140.6 %reduce-scatter.5.cloned.1.call-start = ((), (), s32[]{:S(2)}) async-start(), calls=%async_computation.5 | async-start | bytes 1966080 | tf_op jit(solution)/shard_map/reduce_scatter | solution.py:179
  315.2 1.0 copy-start.12
  315.3 130.1 %copy-start.19 = (bf16[3,768,16]{1,2,0:T(8,128)(2,1)S(1)}, bf16[3,768,16]{1,2,0:T(8,128)(2,1)}, u32[]{:S(2)}) copy-start(bf16[3,768,16]{1,2,0:T(8,128)(2,1)} %param.15) | copy-start | bytes 221188
Sparse Core Ops, SparseCore 0:
  9.7 29.7 all-gather.6
  41.1 26.5 all-gather.8
  70.6 53.4 all-gather.10
  189.1 54.7 all-gather.12
  246.1 23.7 reduce-scatter.2
  304.9 100.3 all-reduce.4
  407.8 23.5 reduce-scatter.4
where the time goes:
time: 461 us; the launch traced here: 454 us
  blocking collectives  161 us (35%)
  waiting for transfers between devices  126 us (27%)
  other arithmetic  85.3 us (19%)
  matrix products  57.6 us (12%)
  between operations  14.5 us (3%)
  local copies, waits for them, and re-layouts  8.28 us (2%)
    psum x1, blocking collectives, on_device(): lax.psum(part_down_out.astype(jnp.bfloat16), 'ctx').astype(jnp.float32)  122 us
    all_gather x2, waiting for transfers between devices, entering(): everything = lax.all_gather(array.astype(jnp.bfloat16), axis)  92.6 us
    select_n x64, other arithmetic, hop(): return jnp.where(reached, new, before)  79.1 us
    all_gather x1, waiting for transfers between devices, on_device(): segment = lax.all_gather(tokens, 'head', axis=1, tiled=True)  19 us
    psum x1, blocking collectives, on_device(): lax.psum(jnp.dot(attended_output, output_down_weight, preferred_element_t...  13.3 us
    psum x1, blocking collectives, on_device(): backward_low_rank = lax.psum(low_part.astype(jnp.bfloat16), 'head')  13.3 us
    all_gather x1, waiting for transfers between devices, on_device(): lax.all_gather(cotangent, 'head', axis=1, tiled=True)  12.8 us
    all_gather x1, blocking collectives, on_device(): d_rows = lax.all_gather(input_down_weights, 'head', axis=1, tiled=True)  11.8 us
  transfers between devices with their start and end apart: 7, of which 4 were waited for; matrix products, arithmetic and copies ran while one was open for 21% of the time, Pallas kernels for 0%

commit v1 on v0

v1 whole, which is shorter than its diff:
```python
import functools

import jax
import jax.numpy as jnp
from jax import lax
from jax.experimental import pallas as pl
from jax.experimental.pallas import tpu as pltpu
from jax.sharding import PartitionSpec as P

HEAD_DIM = 128
RANK = 16
PAIR = 2 * HEAD_DIM
adapter_scale = 0.5
epsilon = 1e-06
bf16 = jnp.bfloat16
f32 = jnp.float32
VMEM_BYTES = 24 * 2**20

NN = (((1,), (0,)), ((), ()))
NT = (((1,), (1,)), ((), ()))
TN = (((0,), (0,)), ((), ()))


def mm(a, b, dims=NN):
    return lax.dot_general(a, b, dims, preferred_element_type=f32)


def call(kernel, grid, in_specs, out_specs, out_shape, flops, moved, prefetch=0):
    return pl.pallas_call(
        kernel,
        grid_spec=pltpu.PrefetchScalarGridSpec(
            num_scalar_prefetch=prefetch, grid=grid, in_specs=in_specs, out_specs=out_specs
        ),
        out_shape=out_shape,
        compiler_params=pltpu.CompilerParams(
            dimension_semantics=("arbitrary",) * len(grid), vmem_limit_bytes=VMEM_BYTES
        ),
        cost_estimate=pl.CostEstimate(flops=flops, bytes_accessed=moved, transcendentals=0),
    )


def whole(shape):
    return pl.BlockSpec(shape, lambda *_: (0,) * len(shape))


def struct(shape, dtype):
    return jax.ShapeDtypeStruct(shape, dtype)


def project_kernel(chunks, with_sum, idx_ref, *refs):
    toks, weights = refs[:chunks], refs[chunks : 2 * chunks]
    total_ref = refs[2 * chunks] if with_sum else None
    out_ref = refs[-1]
    for m in range(3):
        total = mm(toks[0][...], weights[0][m])
        for c in range(1, chunks):
            total = total + mm(toks[c][...], weights[c][m])
        if with_sum:
            total = total + total_ref[m]
        out_ref[m] = total


def weight_specs(count, width):
    return [
        pl.BlockSpec((3, width, PAIR), functools.partial(lambda c, i, idx: (0, idx[c], i), c))
        for c in range(count)
    ]


def project(idx, toks, weight, total=None):
    count = len(toks)
    rows, width = toks[0].shape
    cols = weight.shape[2]
    tile = pl.BlockSpec((3, rows, PAIR), lambda i, idx: (0, 0, i))
    in_specs = [whole((rows, width))] * count + weight_specs(count, width)
    operands = list(toks) + [weight] * count
    if total is not None:
        in_specs.append(tile)
        operands.append(total)
    return call(
        functools.partial(project_kernel, count, total is not None),
        (cols // PAIR,),
        in_specs,
        tile,
        struct((3, rows, cols), f32),
        6 * rows * width * cols * count,
        6 * width * cols * count + 24 * rows * cols,
        prefetch=1,
    )(idx, *operands)


def project_last_kernel(idx_ref, tok_ref, weight_ref, total_ref, low_ref, up_ref, out_ref, state_ref):
    parts = []
    for m in range(3):
        total = mm(tok_ref[...], weight_ref[m]) + total_ref[m]
        total = total + adapter_scale * mm(low_ref[m], up_ref[m])
        part = total.astype(bf16)
        out_ref[m] = part
        parts.append(part)
    for h in range(2):
        at = slice(h * HEAD_DIM, (h + 1) * HEAD_DIM)
        state_ref[h] = mm(parts[1][:, at], parts[2][:, at], TN)


def project_last(idx, tok, weight, total, low, up):
    rows, width = tok.shape
    cols = weight.shape[2]
    tile = pl.BlockSpec((3, rows, PAIR), lambda i, idx: (0, 0, i))
    return call(
        project_last_kernel,
        (cols // PAIR,),
        [whole((rows, width))]
        + weight_specs(1, width)
        + [tile, whole((3, rows, RANK)), pl.BlockSpec((3, RANK, PAIR), lambda i, idx: (0, 0, i))],
        [tile, pl.BlockSpec((2, HEAD_DIM, HEAD_DIM), lambda i, idx: (i, 0, 0))],
        [struct((3, rows, cols), bf16), struct((cols // HEAD_DIM, HEAD_DIM, HEAD_DIM), f32)],
        6 * rows * width * cols,
        6 * width * cols + 18 * rows * cols,
        prefetch=1,
    )(idx, tok, weight, total, low, up)


def attended_gradient_kernel(idx_ref, *refs):
    cots, weights = refs[:4], refs[4:8]
    back_ref, down_ref, out_ref = refs[8:]
    total = adapter_scale * mm(back_ref[...], down_ref[...])
    for c in range(4):
        total = total + mm(cots[c][...], weights[c][...], NT)
    out_ref[...] = total


def attended_gradient(idx, cots, weight, back_mid, down_out):
    rows, width = cots[0].shape
    cols = weight.shape[0]
    return call(
        attended_gradient_kernel,
        (cols // PAIR,),
        [whole((rows, width))] * 4
        + [
            pl.BlockSpec((PAIR, width), functools.partial(lambda c, i, idx: (i, idx[c]), c))
            for c in range(4)
        ]
        + [whole((rows, RANK)), pl.BlockSpec((RANK, PAIR), lambda i, idx: (0, i))],
        pl.BlockSpec((rows, PAIR), lambda i, idx: (0, i)),
        struct((rows, cols), f32),
        8 * rows * width * cols,
        8 * width * cols + 8 * rows * width + 4 * rows * cols,
        prefetch=1,
    )(idx, *cots, *([weight] * 4), back_mid, down_out)


def lower_mask(rows):
    s = lax.broadcasted_iota(jnp.int32, (rows, rows), 0)
    t = lax.broadcasted_iota(jnp.int32, (rows, rows), 1)
    return s >= t


def forward_kernel(
    qkv_ref, held_ref, grad_ref, back_ref, down_ref, att_ref, draw_ref, state_ref, mid_ref, gdown_ref
):
    rows = att_ref.shape[0]
    mask = lower_mask(rows)

    @pl.when(pl.program_id(0) == 0)
    def _():
        mid_ref[...] = jnp.zeros_like(mid_ref)

    for h in range(2):
        at = slice(h * HEAD_DIM, (h + 1) * HEAD_DIM)
        q, k, v = (qkv_ref[m, :, at] for m in range(3))
        scores = jnp.where(mask, mm(q, k, NT), 0.0).astype(bf16)
        raw = mm(scores, v) + mm(q, held_ref[h])
        inverse = 1.0 / jnp.sqrt(jnp.mean(raw * raw, axis=-1, keepdims=True) + epsilon)
        normed = raw * inverse
        att = normed.astype(bf16)
        grad = grad_ref[:, at]
        along = jnp.mean(grad * normed, axis=-1, keepdims=True)
        draw = ((grad - normed * along) * inverse).astype(bf16)
        att_ref[:, at] = att
        draw_ref[:, at] = draw
        state_ref[h] = mm(q, draw, TN)
        gdown_ref[h] = mm(back_ref[...], att)
        mid_ref[...] += mm(att, down_ref[:, at], NT)


def forward_heads(qkv, held, grad, back_mid_t, down_out):
    _, rows, cols = qkv.shape
    heads = cols // HEAD_DIM
    tile = pl.BlockSpec((rows, PAIR), lambda i: (0, i))
    state = pl.BlockSpec((2, HEAD_DIM, HEAD_DIM), lambda i: (i, 0, 0))
    return call(
        forward_kernel,
        (cols // PAIR,),
        [
            pl.BlockSpec((3, rows, PAIR), lambda i: (0, 0, i)),
            state,
            tile,
            whole((RANK, rows)),
            pl.BlockSpec((RANK, PAIR), lambda i: (0, i)),
        ],
        [
            tile,
            tile,
            state,
            whole((rows, RANK)),
            pl.BlockSpec((2, RANK, HEAD_DIM), lambda i: (i, 0, 0)),
        ],
        [
            struct((rows, cols), bf16),
            struct((rows, cols), bf16),
            struct((heads, HEAD_DIM, HEAD_DIM), f32),
            struct((rows, RANK), f32),
            struct((heads, RANK, HEAD_DIM), f32),
        ],
        4 * rows * cols * (2 * rows + 2 * HEAD_DIM),
        14 * rows * cols,
    )(qkv, held, grad, back_mid_t, down_out)


def within_kernel(
    qkv_ref, held_ref, draw_ref, low_ref, up_ref, dq_ref, dk_ref, dv_ref, back_ref, gup_ref
):
    rows = draw_ref.shape[0]
    mask = lower_mask(rows)

    @pl.when(pl.program_id(0) == 0)
    def _():
        back_ref[...] = jnp.zeros_like(back_ref)

    for h in range(2):
        at = slice(h * HEAD_DIM, (h + 1) * HEAD_DIM)
        q, k, v = (qkv_ref[m, :, at] for m in range(3))
        draw = draw_ref[:, at]
        scores = jnp.where(mask, mm(q, k, NT), 0.0).astype(bf16)
        dscores = jnp.where(mask, mm(draw, v, NT), 0.0).astype(bf16)
        dq = (mm(dscores, k) + mm(draw, held_ref[h], NT)).astype(bf16)
        dq_ref[:, at] = dq
        dk_ref[:, at] = mm(dscores, q, TN)
        dv_ref[:, at] = mm(scores, draw, TN)
        back_ref[...] += mm(dq, up_ref[:, at], NT)
        gup_ref[h] = mm(low_ref[...], dq)


def within_block(qkv, held, draw, low_t, up):
    _, rows, cols = qkv.shape
    heads = cols // HEAD_DIM
    tile = pl.BlockSpec((rows, PAIR), lambda i: (0, i))
    return call(
        within_kernel,
        (cols // PAIR,),
        [
            pl.BlockSpec((3, rows, PAIR), lambda i: (0, 0, i)),
            pl.BlockSpec((2, HEAD_DIM, HEAD_DIM), lambda i: (i, 0, 0)),
            tile,
            whole((RANK, rows)),
            pl.BlockSpec((RANK, PAIR), lambda i: (0, i)),
        ],
        [
            tile,
            tile,
            tile,
            whole((rows, RANK)),
            pl.BlockSpec((2, RANK, HEAD_DIM), lambda i: (i, 0, 0)),
        ],
        [
            struct((rows, cols), bf16),
            struct((rows, cols), f32),
            struct((rows, cols), f32),
            struct((rows, RANK), f32),
            struct((heads, RANK, HEAD_DIM), f32),
        ],
        4 * rows * cols * (5 * rows + HEAD_DIM),
        18 * rows * cols,
    )(qkv, held, draw, low_t, up)


def across_kernel(
    qkv_ref, suffix_ref, dk_ref, dv_ref, low_ref, up_ref, out_ref, back_ref, gup_ref
):
    @pl.when(pl.program_id(0) == 0)
    def _():
        back_ref[...] = jnp.zeros_like(back_ref)

    for h in range(2):
        at = slice(h * HEAD_DIM, (h + 1) * HEAD_DIM)
        k, v = qkv_ref[1, :, at], qkv_ref[2, :, at]
        held = suffix_ref[h]
        dk = (dk_ref[:, at] + mm(v, held, NT)).astype(bf16)
        dv = (dv_ref[:, at] + mm(k, held)).astype(bf16)
        for m, part in ((0, dk), (1, dv)):
            out_ref[m, :, at] = part
            back_ref[m] += mm(part, up_ref[m + 1, :, at], NT)
            gup_ref[m, h] = mm(low_ref[m + 1], part)


def across_blocks(qkv, suffix, dk, dv, low_t, up):
    _, rows, cols = qkv.shape
    heads = cols // HEAD_DIM
    tile = pl.BlockSpec((rows, PAIR), lambda i: (0, i))
    return call(
        across_kernel,
        (cols // PAIR,),
        [
            pl.BlockSpec((3, rows, PAIR), lambda i: (0, 0, i)),
            pl.BlockSpec((2, HEAD_DIM, HEAD_DIM), lambda i: (i, 0, 0)),
            tile,
            tile,
            whole((3, RANK, rows)),
            pl.BlockSpec((3, RANK, PAIR), lambda i: (0, 0, i)),
        ],
        [
            pl.BlockSpec((2, rows, PAIR), lambda i: (0, 0, i)),
            whole((2, rows, RANK)),
            pl.BlockSpec((2, 2, RANK, HEAD_DIM), lambda i: (0, i, 0, 0)),
        ],
        [
            struct((2, rows, cols), bf16),
            struct((2, rows, RANK), f32),
            struct((2, heads, RANK, HEAD_DIM), f32),
        ],
        8 * rows * cols * HEAD_DIM,
        18 * rows * cols,
    )(qkv, suffix, dk, dv, low_t, up)


def output_kernel(att_ref, weight_ref, out_ref):
    out_ref[0] = mm(att_ref[...], weight_ref[...]).astype(bf16)


def output_parts(att, weight, width):
    rows, cols = att.shape
    parts = weight.shape[1] // width
    return call(
        output_kernel,
        (parts,),
        [whole((rows, cols)), pl.BlockSpec((cols, width), lambda i: (0, i))],
        pl.BlockSpec((1, rows, width), lambda i: (i, 0, 0)),
        struct((parts, rows, width), bf16),
        2 * rows * cols * width * parts,
        2 * cols * width * parts,
    )(att, weight)


def input_kernel(idx_ref, dq_ref, dkv_ref, weight_ref, out_ref):
    total = mm(dq_ref[...], weight_ref[0], NT)
    for m in range(2):
        total = total + mm(dkv_ref[m], weight_ref[m + 1], NT)
    out_ref[...] = total.astype(out_ref.dtype)


def input_part(idx, dq, dkv, weight, width, dtype):
    rows, cols = dq.shape
    tiles = width // 256
    return call(
        input_kernel,
        (tiles,),
        [
            whole((rows, cols)),
            whole((2, rows, cols)),
            pl.BlockSpec((3, 256, cols), lambda i, idx: (0, idx[0] * tiles + i, 0)),
        ],
        pl.BlockSpec((rows, 256), lambda i, idx: (0, i)),
        struct((rows, width), dtype),
        6 * rows * cols * width,
        6 * cols * width + 6 * rows * cols,
        prefetch=1,
    )(idx, dq, dkv, weight)


def shift(array, by):
    n = lax.axis_size("head")
    return lax.ppermute(array, "head", [(i, (i + by) % n) for i in range(n)])


def sum_over_head(part):
    sent = part.astype(bf16)
    total = part
    for by in (2, 1, 3):
        total = total + shift(sent, by).astype(f32)
    return total


def swap_cores(array):
    n = lax.axis_size("ctx")
    return lax.ppermute(array, "ctx", [(i, i ^ 1) for i in range(n)])


def scan_states(state, reverse):
    n = lax.axis_size("ctx")
    chips = n // 2
    groups = [[core + 2 * chip for chip in range(chips)] for core in range(2)]
    heads = state.shape[0]
    half = heads // 2
    core = lax.axis_index("ctx") % 2
    first = core == (1 if reverse else 0)
    mine = lax.dynamic_slice_in_dim(state, core * half, half)
    given = lax.dynamic_slice_in_dim(state, (1 - core) * half, half)
    got = swap_cores(given.astype(bf16)).astype(f32)
    pair = (mine + got).astype(bf16).reshape(chips, -1, HEAD_DIM)
    every = lax.all_to_all(pair, "ctx", 0, 0, axis_index_groups=groups).astype(f32)
    before = jnp.cumsum(every, axis=0, dtype=f32)
    before = before[-1:] - before if reverse else before - every
    chip = lax.all_to_all(before.astype(bf16), "ctx", 0, 0, axis_index_groups=groups)
    chip = chip.reshape(mine.shape).astype(f32)
    own = jnp.where(first, chip, chip + got).astype(bf16)
    other = jnp.where(first, chip + mine, chip).astype(bf16)
    back = swap_cores(other)
    low = jnp.where(core == 0, own, back)
    high = jnp.where(core == 0, back, own)
    return jnp.concatenate([low, high])


def sum_over_ctx(parts):
    n = lax.axis_size("ctx")
    flat = parts.astype(bf16).reshape(n, -1, HEAD_DIM)
    every = lax.all_to_all(flat, "ctx", 0, 0).astype(f32)
    total = jnp.sum(every, axis=0).astype(bf16)
    spread = jnp.broadcast_to(total[None], flat.shape)
    return lax.all_to_all(spread, "ctx", 0, 0).reshape(parts.shape).astype(f32)


def blocks_of(rows):
    wide = rows.shape[-1] // HEAD_DIM
    return rows.reshape(RANK, wide, HEAD_DIM).transpose(1, 0, 2)


def rows_of(blocks):
    return blocks.transpose(1, 0, 2).reshape(RANK, -1)


def on_device(
    tokens,
    query_key_value_weight,
    output_weight,
    input_down_weights,
    input_up_weights,
    output_down_weight,
    output_up_weight,
    cotangent,
):
    rows, width = tokens.shape
    cols = query_key_value_weight.shape[2]
    heads = cols // HEAD_DIM
    me = lax.axis_index("head").astype(jnp.int32)
    parts = lax.axis_size("head")
    scale_factor = adapter_scale * (rows * lax.axis_size("ctx")) ** (-0.5)

    def index(*shifts):
        return jnp.stack([(me + s) % parts for s in shifts])

    down_t = input_down_weights.transpose(0, 2, 1).reshape(3 * RANK, width)
    down_out_t = output_down_weight.T

    from2, from1, from3 = shift(tokens, 2), shift(tokens, 1), shift(tokens, 3)

    low_part = mm(tokens, down_t, NT)
    back_part = mm(cotangent, output_up_weight, NT)
    low_all = sum_over_head(jnp.concatenate([low_part, back_part], axis=1)).astype(bf16)
    low = low_all[:, : 3 * RANK].reshape(rows, 3, RANK).transpose(1, 0, 2)
    low_t = low.transpose(0, 2, 1)
    back_mid = low_all[:, 3 * RANK :]

    total = project(index(0), [tokens], query_key_value_weight)
    total = project(index(-1, -3), [from1, from3], query_key_value_weight, total)
    qkv, kv_total = project_last(
        index(-2), from2, query_key_value_weight, total, low, input_up_weights
    )

    cots = [cotangent] + [shift(cotangent, s) for s in (2, 1, 3)]
    held = scan_states(kv_total, False)
    grad = attended_gradient(index(0, -2, -1, -3), cots, output_weight, back_mid, down_out_t)

    attended, d_raw, qd_total, mid_part, gdown_out = forward_heads(
        qkv, held, grad, back_mid.T, down_out_t
    )
    suffix = scan_states(qd_total, True)

    mid = sum_over_head(mid_part).astype(bf16)
    dq, dk_within, dv_within, back_q, gup_q = within_block(
        qkv, held, d_raw, low_t[0], input_up_weights[0]
    )
    out_parts = output_parts(attended, output_weight, width)
    out_every = lax.all_to_all(out_parts, "head", 0, 0)
    output = (
        jnp.sum(out_every.astype(f32), axis=0) + adapter_scale * mm(mid, output_up_weight)
    ).astype(bf16)
    gup_out = mm(mid, cotangent, TN)

    dkv, back_kv, gup_kv = across_blocks(
        qkv, suffix, dk_within, dv_within, low_t, input_up_weights
    )
    back_low = sum_over_head(jnp.concatenate([back_q, back_kv[0], back_kv[1]], axis=1)).astype(bf16)
    grad_parts = []
    for s in (2, 1, 3):
        part = input_part(index(s), dq, dkv, query_key_value_weight, width, bf16)
        grad_parts.append(shift(part, s))
    grad_sum = input_part(index(0), dq, dkv, query_key_value_weight, width, f32)
    grad_sum = grad_sum + adapter_scale * mm(back_low, down_t)
    for part in grad_parts:
        grad_sum = grad_sum + part.astype(f32)
    input_grad = grad_sum.astype(bf16)

    gdown = mm(back_low, tokens, TN).reshape(3, RANK, width)
    wide = width // HEAD_DIM
    sums = sum_over_ctx(
        jnp.concatenate(
            [blocks_of(gdown[m]) for m in range(3)]
            + [blocks_of(gup_out), gdown_out, gup_q, gup_kv[0], gup_kv[1]]
        )
    )
    sums = scale_factor * sums
    grad_down_qkv = jnp.stack(
        [rows_of(sums[m * wide : (m + 1) * wide]).T for m in range(3)]
    )
    at = 3 * wide
    grad_up_out = rows_of(sums[at : at + wide])
    at += wide
    grad_down_out = rows_of(sums[at : at + heads]).T
    at += heads
    grad_up_qkv = jnp.stack(
        [rows_of(sums[at + m * heads : at + (m + 1) * heads]) for m in range(3)]
    )
    return (output, input_grad, grad_down_qkv, grad_up_qkv, grad_down_out, grad_up_out)


def solution(mesh):
    return jax.shard_map(
        on_device,
        mesh=mesh,
        in_specs=(
            P("ctx", "head"),
            P(None, None, "head"),
            P("head", None),
            P(None, "head", None),
            P(None, None, "head"),
            P("head", None),
            P(None, "head"),
            P("ctx", "head"),
        ),
        out_specs=(
            P("ctx", "head"),
            P("ctx", "head"),
            P(None, "head", None),
            P(None, None, "head"),
            P("head", None),
            P(None, "head"),
        ),
        check_vma=False,
    )
```

time: 461 us -> 229 us (0.50); the launches traced: 454 us -> 227 us
  blocking collectives: 161 us -> 0 us
  waiting for transfers between devices: 126 us -> 39.8 us
  starting transfers between devices: 0.46 us -> 71.3 us
  other arithmetic: 85.3 us -> 17 us
  matrix products: 57.6 us -> 5.61 us
  Pallas kernels: 0 us -> 44.8 us
  local copies, waits for them, and re-layouts: 8.28 us -> 47.1 us
  between operations: 14.5 us -> 1.42 us
    psum x3 -> x0, blocking collectives: 149 us -> none  [the longest x1 122 us: on_device(): lax.psum(part_down_out.astype(jnp.bfloat16), 'ctx').astype(jnp.float32)]
    all_gather x4 -> x0, waiting for transfers between devices: 124 us -> none  [the longest x2 92.6 us: entering(): everything = lax.all_gather(array.astype(jnp.bfloat16), axis)]
    select_n x64 -> x2, other arithmetic: 79.1 us -> 2.06 us  [scan_states(): low = jnp.where(core == 0, own, back)]
    dot_general x28 -> x6, matrix products: 57.6 us -> 5.61 us  [mm(): return lax.dot_general(a, b, dims, preferred_element_type=f32)]
    pallas_call x0 -> x12, Pallas kernels: none -> 44.8 us  [the longest x4 9.55 us: input_part(): call(input_kernel, (tiles,), [whole((rows, cols)), whole((2, rows, cols))...]
    all_to_all x0 -> x7, waiting for transfers between devices: none -> 39.6 us  [the longest x1 15.1 us: on_device(): out_every = lax.all_to_all(out_parts, 'head', 0, 0)]
    all_to_all x0 -> x7, starting transfers between devices: none -> 39.1 us  [the longest x2 11.8 us: scan_states(): lax.all_to_all(pair, 'ctx', 0, 0, axis_index_groups=groups).astype(f32)]
    unnamed x40 -> x70, local copies, waits for them, and re-layouts: 3.38 us -> 39.2 us
  transfers between devices with their start and end apart: 7 -> 29, of which waited for: 4 -> 6; matrix products, arithmetic and copies ran while one was open for 21% -> 11% of each run, Pallas kernels for 0% -> 14%
where the time goes in v1:
time: 229 us; the launch traced here: 227 us
  starting transfers between devices  71.3 us (31%)
  local copies, waits for them, and re-layouts  47.1 us (21%)
  Pallas kernels  44.8 us (20%)
  waiting for transfers between devices  39.8 us (17%)
  other arithmetic  17 us (7%)
  matrix products  5.61 us (2%)
    unnamed x70, local copies, waits for them, and re-layouts  39.2 us
    ppermute x18, starting transfers between devices, shift(): return lax.ppermute(array, 'head', [(i, (i + by) % n) for i in range(n)])  23.4 us
    all_to_all x1, waiting for transfers between devices, on_device(): out_every = lax.all_to_all(out_parts, 'head', 0, 0)  15.1 us
    all_to_all x2, starting transfers between devices, scan_states(): lax.all_to_all(pair, 'ctx', 0, 0, axis_index_groups=groups).astype(f32)  11.8 us
    all_to_all x2, starting transfers between devices, scan_states(): lax.all_to_all(before.astype(bf16), 'ctx', 0, 0, axis_index_groups=groups)  10.7 us
    all_to_all x2, waiting for transfers between devices, scan_states(): lax.all_to_all(before.astype(bf16), 'ctx', 0, 0, axis_index_groups=groups)  10.6 us
    pallas_call x4, Pallas kernels, input_part(): call(input_kernel, (tiles,), [whole((rows, cols)), whole((2, rows, cols))...  9.55 us
    pallas_call x2, Pallas kernels, project(): call(functools.partial(project_kernel, count, total is not None), (cols /...  9.01 us
  transfers between devices with their start and end apart: 29, of which 6 were waited for; matrix products, arithmetic and copies ran while one was open for 11% of the time, Pallas kernels for 14%

profile of v1, /device:TPU:1, one launch (start us, length us, event | category | flops | bytes accessed | tf_op | source)
XLA Modules:
  0.0 227.2 jit_solution(9802201586695471819)
XLA Ops:
  0.6 2.2 collective-permute-start.1
  2.8 1.5 collective-permute-start.2
  6.9 1.6 collective-permute-start.3
  9.0 2.3 %collective-permute-start.5 = (bf16[256,64]{0,1:T(8,128)(2,1)S(1)}, bf16[256,64]{0,1:T(8,128)(2,1)S(1)}, u32[]{:S(2)}, u32[]{:S(2)}) collective-permute-start(bf16[256,64]{0,1:T(8,128)(2,1)S(1)} %fusion.13), channel_id=1, source_target_pairs={{0,3},{1,0},{2,1},{3,2},{4,7},{5,4},{6,5},{7,6},{8,11},{9,8},{10,9... | collective-permute-start | bytes 98312 | tf_op jit(solution)/shard_map/ppermute | solution.py:372
  11.2 6.4 %copy-done.1 = bf16[3,3072,1024]{2,1,0:T(8,128)(2,1)S(1)} copy-done((bf16[3,3072,1024]{2,1,0:T(8,128)(2,1)S(1)}, bf16[3,3072,1024]{2,1,0:T(8,128)(2,1)}, u32[]{:S(2)}) %copy-start.1) | copy-done | bytes 18874392
  18.6 2.8 %shard_map.127.refs_4_ = f32[3,256,1024]{2,1,0:T(8,128)S(1)} custom-call(s32[1]{0:T(128)} %bitcast.3.idx_ref, bf16[256,768]{1,0:T(8,128)(2,1)S(1)} %copy-done.8, bf16[3,3072,1024]{2,1,0:T(8,128)(2,1)S(1)} %copy-done.1), custom_call_target="tpu_custom_call" | custom-call | flops 1207959552 | bytes 11010048 | tf_op jit(solution)/shard_map/pallas_call | solution.py:80
  22.6 6.4 %copy-done.2 = bf16[3,3072,1024]{2,1,0:T(8,128)(2,1)S(1)} copy-done((bf16[3,3072,1024]{2,1,0:T(8,128)(2,1)S(1)}, bf16[3,3072,1024]{2,1,0:T(8,128)(2,1)}, u32[]{:S(2)}) %copy-start.2) | copy-done | bytes 18874392
  29.0 6.2 %shard_map.128.total_ref = f32[3,256,1024]{2,1,0:T(8,128)S(1)} custom-call(s32[2]{0:T(128)S(1)} %pad_add_fusion.idx_ref, bf16[256,768]{1,0:T(8,128)(2,1)} %collective-permute-done.1.refs_0_, bf16[256,768]{1,0:T(8,128)(2,1)} %collective-permute-done.2.refs_1_, bf16[3,3072,1024]{2,1,0:T(8,128)(2,1)S(1)} %copy-done.2, bf16[3,3072,1024]{2,1,0:T(8,128)(2,1)S(1)} %copy-done.2, ...), custom_call_target="tpu_custom_call" | custom-call | flops 2415919104 | bytes 15728640 | tf_op jit(solution)/shard_map/pallas_call | solution.py:80
  35.2 4.9 %shard_map.129 = (bf16[3,256,1024]{2,1,0:T(8,128)(2,1)S(1)}, f32[8,128,128]{2,1,0:T(8,128)S(1)}) custom-call(s32[1]{0:T(128)} %bitcast.idx_ref, bf16[256,768]{1,0:T(8,128)(2,1)} %collective-permute-done.tok_ref, bf16[3,3072,1024]{2,1,0:T(8,128)(2,1)S(1)} %copy-done.2, f32[3,256,1024]{2,1,0:T(8,128)S(1)} %shard_map.128.total_ref, ...), custom_call_target="tpu_custom_call" | custom-call | flops 1207959552 | bytes 9437184 | tf_op jit(solution)/shard_map/pallas_call | solution.py:109
  41.0 2.1 collective-permute-start.6
  43.1 1.6 collective-permute-start.10
  44.7 1.4 collective-permute-start.8
  46.9 1.6 fusion.4
  48.5 7.6 %all-to-all-start = ((bf16[16,32,128]{2,1,0:T(8,128)(2,1)}), bf16[16,32,128]{2,1,0:T(8,128)(2,1)}, u32[]{:S(2)}, u32[]{:S(2)}) async-start(bf16[16,32,128]{2,1,0:T(8,128)(2,1)} %bitcast.169), calls=%async_computation | async-start | bytes 262144 | tf_op jit(solution)/shard_map/all_to_all | solution.py:400
  56.9 6.2 %all-to-all-done = bf16[16,32,128]{2,1,0:T(8,128)(2,1)} async-done(((bf16[16,32,128]{2,1,0:T(8,128)(2,1)}), bf16[16,32,128]{2,1,0:T(8,128)(2,1)}, u32[]{:S(2)}, u32[]{:S(2)}) %all-to-all-start) | async-done | bytes 131104 | tf_op jit(solution)/shard_map/all_to_all | solution.py:400
  63.1 1.8 fusion.2
  64.8 4.2 %all-to-all-start.1 = ((bf16[16,32,128]{2,1,0:T(8,128)(2,1)}), bf16[16,32,128]{2,1,0:T(8,128)(2,1)}, u32[]{:S(2)}, u32[]{:S(2)}) async-start(bf16[16,32,128]{2,1,0:T(8,128)(2,1)} %fusion.2), calls=%async_computation.1 | async-start | bytes 262144 | tf_op jit(solution)/shard_map/all_to_all | solution.py:403
  69.0 1.3 slice_bitcast_fusion.18
  71.1 4.8 %all-to-all-done.1 = bf16[16,32,128]{2,1,0:T(8,128)(2,1)} async-done(((bf16[16,32,128]{2,1,0:T(8,128)(2,1)}), bf16[16,32,128]{2,1,0:T(8,128)(2,1)}, u32[]{:S(2)}, u32[]{:S(2)}) %all-to-all-start.1) | async-done | bytes 131104 | tf_op jit(solution)/shard_map/all_to_all | solution.py:403
  76.8 3.5 %collective-permute-start.7 = (bf16[4,128,128]{2,1,0:T(8,128)(2,1)S(1)}, bf16[4,128,128]{2,1,0:T(8,128)(2,1)S(1)}, u32[]{:S(2)}, u32[]{:S(2)}) collective-permute-start(bf16[4,128,128]{2,1,0:T(8,128)(2,1)S(1)} %fusion.7), channel_id=1, source_target_pairs={{0,4},{4,0},{8,12},{12,8},{16,20},{20,16},{24,28},{28,24},{32,36},... | collective-permute-start | bytes 393224 | tf_op jit(solution)/shard_map/ppermute | solution.py:385
  80.3 2.8 %copy-done.5 = bf16[1024,3072]{1,0:T(8,128)(2,1)S(1)} copy-done((bf16[1024,3072]{1,0:T(8,128)(2,1)S(1)}, bf16[1024,3072]{1,0:T(8,128)(2,1)}, u32[]{:S(2)}) %copy-start.5) | copy-done | bytes 6291480
  83.9 4.5 %shard_map.130.grad_ref = f32[256,1024]{1,0:T(8,128)S(1)} custom-call(s32[4]{0:T(128)S(1)} %pad_add_fusion.1.idx_ref, bf16[256,768]{1,0:T(8,128)(2,1)S(1)} %copy-done.7, bf16[256,768]{1,0:T(8,128)(2,1)S(1)} %collective-permute-done.8.refs_1_, bf16[256,768]{1,0:T(8,128)(2,1)} %collective-permute-done.9.refs_2_, ...), custom_call_target="tpu_custom_call" | custom-call | flops 1610612736 | bytes 8912896 | tf_op jit(solution)/shard_map/pallas_call | solution.py:135
  89.5 6.3 %shard_map.131 = (bf16[256,1024]{1,0:T(8,128)(2,1)S(1)}, bf16[256,1024]{1,0:T(8,128)(2,1)S(1)}, f32[8,128,128]{2,1,0:T(8,128)}, f32[256,16]{1,0:T(8,128)S(1)}, f32[8,16,128]{2,1,0:T(8,128)S(1)}) custom-call(bf16[3,256,1024]{2,1,0:T(8,128)(2,1)S(1)} %get-tuple-element.21.qkv_ref, bf16[8,128,128]{2,1,0:T(8,128)(2,1)S(1)} %pad_maximum_fusion.held_ref, ...), custom_call_target="tpu_custom_call" | custom-call | flops 805306368 | bytes 3670016 | tf_op jit(solution)/shard_map/pallas_call | solution.py:191
  100.7 1.8 collective-permute-start.13
  102.5 1.7 fusion.5
  104.1 4.2 %all-to-all-start.3 = ((bf16[16,32,128]{2,1,0:T(8,128)(2,1)}), bf16[16,32,128]{2,1,0:T(8,128)(2,1)}, u32[]{:S(2)}, u32[]{:S(2)}) async-start(bf16[16,32,128]{2,1,0:T(8,128)(2,1)} %bitcast.16), calls=%async_computation.3 | async-start | bytes 262144 | tf_op jit(solution)/shard_map/all_to_all | solution.py:400
  109.4 4.2 %shard_map.133 = (bf16[256,1024]{1,0:T(8,128)(2,1)S(1)}, f32[256,1024]{1,0:T(8,128)S(1)}, f32[256,1024]{1,0:T(8,128)S(1)}, f32[256,16]{1,0:T(8,128)S(1)}, f32[8,16,128]{2,1,0:T(8,128)S(1)}) custom-call(bf16[3,256,1024]{2,1,0:T(8,128)(2,1)S(1)} %get-tuple-element.21.qkv_ref, bf16[8,128,128]{2,1,0:T(8,128)(2,1)S(1)} %pad_maximum_fusion.held_ref, ...), custom_call_target="tpu_custom_call" | custom-call | flops 1476395008 | bytes 4718592 | tf_op jit(solution)/shard_map/pallas_call | solution.py:248
  118.0 6.5 %all-to-all-start.4 = ((bf16[16,32,128]{2,1,0:T(8,128)(2,1)}), bf16[16,32,128]{2,1,0:T(8,128)(2,1)S(1)}, u32[]{:S(2)}, u32[]{:S(2)}) async-start(bf16[16,32,128]{2,1,0:T(8,128)(2,1)} %subtract_convert_fusion), calls=%async_computation.4 | async-start | bytes 262144 | tf_op jit(solution)/shard_map/all_to_all | solution.py:403
  125.5 5.8 %all-to-all-done.4 = bf16[16,32,128]{2,1,0:T(8,128)(2,1)S(1)} async-done(((bf16[16,32,128]{2,1,0:T(8,128)(2,1)}), bf16[16,32,128]{2,1,0:T(8,128)(2,1)S(1)}, u32[]{:S(2)}, u32[]{:S(2)}) %all-to-all-start.4) | async-done | bytes 131104 | tf_op jit(solution)/shard_map/all_to_all | solution.py:403
  132.5 3.1 %collective-permute-start.15 = (bf16[4,128,128]{2,1,0:T(8,128)(2,1)S(1)}, bf16[4,128,128]{2,1,0:T(8,128)(2,1)S(1)}, u32[]{:S(2)}, u32[]{:S(2)}) collective-permute-start(bf16[4,128,128]{2,1,0:T(8,128)(2,1)S(1)} %fusion.9), channel_id=1, source_target_pairs={{0,4},{4,0},{8,12},{12,8},{16,20},{20,16},{24,28},{28,24},{32,36},... | collective-permute-start | bytes 393224 | tf_op jit(solution)/shard_map/ppermute | solution.py:385
  138.9 2.7 %shard_map.134 = (bf16[2,256,1024]{2,1,0:T(8,128)(2,1)S(1)}, f32[2,256,16]{2,1,0:T(8,128)S(1)}, f32[2,8,16,128]{3,2,1,0:T(8,128)S(1)}) custom-call(bf16[3,256,1024]{2,1,0:T(8,128)(2,1)S(1)} %copy-done.11, bf16[8,128,128]{2,1,0:T(8,128)(2,1)S(1)} %pad_maximum_fusion.1.suffix_ref, f32[256,1024]{1,0:T(8,128)S(1)} %copy-done.13, f32[256,1024]{1,0:T(8,128)S(1)} %copy-done.15, ...), custom_call_target="tpu_custom_call" | custom-call | flops 268435456 | bytes 4718592 | tf_op jit(solution)/shard_map/pallas_call | solution.py:300
  142.8 2.3 collective-permute-start.18
  145.0 6.4 %copy-done.3 = bf16[3,3072,1024]{2,1,0:T(8,128)(2,1)S(1)} copy-done((bf16[3,3072,1024]{2,1,0:T(8,128)(2,1)S(1)}, bf16[3,3072,1024]{2,1,0:T(8,128)(2,1)}, u32[]{:S(2)}) %copy-start.3) | copy-done | bytes 18874392
  151.4 2.2 shard_map.136
  153.6 1.3 collective-permute-start.19
  155.0 2.2 shard_map.137
  157.3 2.9 %shard_map.138 = bf16[256,768]{1,0:T(8,128)(2,1)} custom-call(s32[1]{0:T(128)} %bitcast.26.idx_ref, bf16[256,1024]{1,0:T(8,128)(2,1)S(1)} %get-tuple-element.26.dq_ref, bf16[2,256,1024]{2,1,0:T(8,128)(2,1)S(1)} %get-tuple-element.30.dkv_ref, bf16[3,3072,1024]{2,1,0:T(8,128)(2,1)S(1)} %copy-done.3), custom_call_target="tpu_custom_call" | custom-call | flops 1207959552 | bytes 6291456 | tf_op jit(solution)/shard_map/pallas_call | solution.py:354
  160.2 2.6 %collective-permute-start.21 = (bf16[256,768]{1,0:T(8,128)(2,1)}, bf16[256,768]{1,0:T(8,128)(2,1)}, u32[]{:S(2)}, u32[]{:S(2)}) collective-permute-start(bf16[256,768]{1,0:T(8,128)(2,1)} %shard_map.138), channel_id=1, source_target_pairs={{0,3},{1,0},{2,1},{3,2},{4,7},{5,4},{6,5},{7,6},{8,11},{9,8},{10,9... | collective-permute-start | bytes 1179656 | tf_op jit(solution)/shard_map/ppermute | solution.py:372
  164.0 5.6 %all-to-all-start.5 = ((bf16[32,28,128]{2,1,0:T(8,128)(2,1)}), bf16[32,28,128]{2,1,0:T(8,128)(2,1)S(1)}, u32[]{:S(2)}, u32[]{:S(2)}) async-start(bf16[32,28,128]{2,1,0:T(8,128)(2,1)} %convert_element_type.167), calls=%async_computation.5 | async-start | bytes 524288 | tf_op jit(solution)/shard_map/all_to_all | solution.py:416
  169.6 2.8 %copy-done.6 = bf16[1024,3072]{1,0:T(8,128)(2,1)S(1)} copy-done((bf16[1024,3072]{1,0:T(8,128)(2,1)S(1)}, bf16[1024,3072]{1,0:T(8,128)(2,1)}, u32[]{:S(2)}) %copy-start.6) | copy-done | bytes 6291480
  172.4 3.6 %shard_map.132 = bf16[4,256,768]{2,1,0:T(8,128)(2,1)} custom-call(bf16[256,1024]{1,0:T(8,128)(2,1)S(1)} %copy-done.18, bf16[1024,3072]{1,0:T(8,128)(2,1)S(1)} %copy-done.6), custom_call_target="tpu_custom_call" | custom-call | flops 1610612736 | bytes 6291456 | tf_op jit(solution)/shard_map/pallas_call | solution.py:333
  176.0 6.4 %copy-done.4 = bf16[3,3072,1024]{2,1,0:T(8,128)(2,1)S(1)} copy-done((bf16[3,3072,1024]{2,1,0:T(8,128)(2,1)S(1)}, bf16[3,3072,1024]{2,1,0:T(8,128)(2,1)}, u32[]{:S(2)}) %copy-start.4) | copy-done | bytes 18874392
  182.3 2.2 shard_map.135
  185.4 7.5 %all-to-all-start.6 = ((bf16[32,28,128]{2,1,0:T(8,128)(2,1)}), bf16[32,28,128]{2,1,0:T(8,128)(2,1)S(1)}, u32[]{:S(2)}, u32[]{:S(2)}) async-start(bf16[32,28,128]{2,1,0:T(8,128)(2,1)} %broadcast_in_dim.2), calls=%async_computation.6 | async-start | bytes 524288 | tf_op jit(solution)/shard_map/all_to_all | solution.py:419
  194.0 7.7 %all-to-all-done.6 = bf16[32,28,128]{2,1,0:T(8,128)(2,1)S(1)} async-done(((bf16[32,28,128]{2,1,0:T(8,128)(2,1)}), bf16[32,28,128]{2,1,0:T(8,128)(2,1)S(1)}, u32[]{:S(2)}, u32[]{:S(2)}) %all-to-all-start.6) | async-done | bytes 229408 | tf_op jit(solution)/shard_map/all_to_all | solution.py:419
  201.8 3.6 %all-to-all-start.2 = ((bf16[4,256,768]{2,1,0:T(8,128)(2,1)}), bf16[4,256,768]{2,1,0:T(8,128)(2,1)S(1)}, u32[]{:S(2)}, u32[]{:S(2)}) async-start(bf16[4,256,768]{2,1,0:T(8,128)(2,1)} %shard_map.132), calls=%async_computation.2 | async-start | bytes 3145728 | tf_op jit(solution)/shard_map/all_to_all | solution.py:483
  205.4 2.5 %add_convert_fusion = bf16[256,768]{1,0:T(8,128)(2,1)} fusion(bf16[256,768]{1,0:T(8,128)(2,1)} %collective-permute-done.21, bf16[256,768]{1,0:T(8,128)(2,1)} %collective-permute-done.20, bf16[256,768]{1,0:T(8,128)(2,1)} %collective-permute-done.19, f32[256,768]{1,0:T(8,128)S(1)} %shard_map.135, f32[256,768]{1,0:T(8,128)} %convolution_multiply_fusion), kind=kLoop, calls=%fused_computation.10 | loop fusion | flops 1572864 | bytes 3145728 | tf_op jit(solution)/shard_map/convert_element_type | solution.py:501
  210.9 15.1 %all-to-all-done.2 = bf16[4,256,768]{2,1,0:T(8,128)(2,1)S(1)} async-done(((bf16[4,256,768]{2,1,0:T(8,128)(2,1)}), bf16[4,256,768]{2,1,0:T(8,128)(2,1)S(1)}, u32[]{:S(2)}, u32[]{:S(2)}) %all-to-all-start.2) | async-done | bytes 1572896 | tf_op jit(solution)/shard_map/all_to_all | solution.py:483
  (153 shorter events, 35.0 us)
Async XLA Ops:
  0.6 21.9 %collective-permute-start.1 = (bf16[256,768]{1,0:T(8,128)(2,1)}, bf16[256,768]{1,0:T(8,128)(2,1)}, u32[]{:S(2)}, u32[]{:S(2)}) collective-permute-start(bf16[256,768]{1,0:T(8,128)(2,1)} %refs_0_.2), channel_id=1, source_target_pairs={{0,1},{1,2},{2,3},{3,0},{4,5},{5,6},{6,7},{7,4},{8,9},{9,10},{10,1... | collective-permute-start | bytes 1179656 | tf_op jit(solution)/shard_map/ppermute | solution.py:372
  2.8 19.8 %collective-permute-start.2 = (bf16[256,768]{1,0:T(8,128)(2,1)}, bf16[256,768]{1,0:T(8,128)(2,1)}, u32[]{:S(2)}, u32[]{:S(2)}) collective-permute-start(bf16[256,768]{1,0:T(8,128)(2,1)} %refs_0_.2), channel_id=1, source_target_pairs={{0,3},{1,0},{2,1},{3,2},{4,7},{5,4},{6,5},{7,6},{8,11},{9,8},{10,9... | collective-permute-start | bytes 1179656 | tf_op jit(solution)/shard_map/ppermute | solution.py:372
  6.9 14.6 %collective-permute-start.3 = (bf16[256,64]{0,1:T(8,128)(2,1)S(1)}, bf16[256,64]{0,1:T(8,128)(2,1)S(1)}, u32[]{:S(2)}, u32[]{:S(2)}) collective-permute-start(bf16[256,64]{0,1:T(8,128)(2,1)S(1)} %fusion.13), channel_id=1, source_target_pairs={{0,2},{1,3},{2,0},{3,1},{4,6},{5,7},{6,4},{7,5},{8,10},{9,11},{10,... | collective-permute-start | bytes 98312 | tf_op jit(solution)/shard_map/ppermute | solution.py:372
  8.6 13.2 %collective-permute-start.4 = (bf16[256,64]{0,1:T(8,128)(2,1)S(1)}, bf16[256,64]{0,1:T(8,128)(2,1)S(1)}, u32[]{:S(2)}, u32[]{:S(2)}) collective-permute-start(bf16[256,64]{0,1:T(8,128)(2,1)S(1)} %fusion.13), channel_id=1, source_target_pairs={{0,1},{1,2},{2,3},{3,0},{4,5},{5,6},{6,7},{7,4},{8,9},{9,10},{10,1... | collective-permute-start | bytes 98312 | tf_op jit(solution)/shard_map/ppermute | solution.py:372
  9.0 12.8 %collective-permute-start.5 = (bf16[256,64]{0,1:T(8,128)(2,1)S(1)}, bf16[256,64]{0,1:T(8,128)(2,1)S(1)}, u32[]{:S(2)}, u32[]{:S(2)}) collective-permute-start(bf16[256,64]{0,1:T(8,128)(2,1)S(1)} %fusion.13), channel_id=1, source_target_pairs={{0,3},{1,0},{2,1},{3,2},{4,7},{5,4},{6,5},{7,6},{8,11},{9,8},{10,9... | collective-permute-start | bytes 98312 | tf_op jit(solution)/shard_map/ppermute | solution.py:372
  11.2 6.4 %copy-start.1 = (bf16[3,3072,1024]{2,1,0:T(8,128)(2,1)S(1)}, bf16[3,3072,1024]{2,1,0:T(8,128)(2,1)}, u32[]{:S(2)}) copy-start(bf16[3,3072,1024]{2,1,0:T(8,128)(2,1)} %weight_ref.11) | copy-start | bytes 56623108
  21.5 13.7 %collective-permute-start = (bf16[256,768]{1,0:T(8,128)(2,1)}, bf16[256,768]{1,0:T(8,128)(2,1)}, u32[]{:S(2)}, u32[]{:S(2)}) collective-permute-start(bf16[256,768]{1,0:T(8,128)(2,1)} %refs_0_.2), channel_id=1, source_target_pairs={{0,2},{1,3},{2,0},{3,1},{4,6},{5,7},{6,4},{7,5},{8,10},{9,11},{10,... | collective-permute-start | bytes 1179656 | tf_op jit(solution)/shard_map/ppermute | solution.py:372
  22.4 12.8 %copy-start.16 = (bf16[3,16,1024]{2,1,0:T(8,128)(2,1)S(1)}, bf16[3,16,1024]{2,1,0:T(8,128)(2,1)}, u32[]{:S(2)}) copy-start(bf16[3,16,1024]{2,1,0:T(8,128)(2,1)} %up_ref.3) | copy-start | bytes 294916
  22.6 6.4 %copy-start.2 = (bf16[3,3072,1024]{2,1,0:T(8,128)(2,1)S(1)}, bf16[3,3072,1024]{2,1,0:T(8,128)(2,1)}, u32[]{:S(2)}) copy-start(bf16[3,3072,1024]{2,1,0:T(8,128)(2,1)} %weight_ref.11) | copy-start | bytes 56623108
  35.2 7.9 %copy-start.7 = (bf16[256,768]{1,0:T(8,128)(2,1)S(1)}, bf16[256,768]{1,0:T(8,128)(2,1)}, u32[]{:S(2)}) copy-start(bf16[256,768]{1,0:T(8,128)(2,1)} %refs_0_.3) | copy-start | bytes 1179652
  40.2 68.2 %copy-start.10 = (bf16[3,256,1024]{2,1,0:T(8,128)(2,1)}, bf16[3,256,1024]{2,1,0:T(8,128)(2,1)S(1)}, u32[]{:S(2)}) copy-start(bf16[3,256,1024]{2,1,0:T(8,128)(2,1)S(1)} %get-tuple-element.21.qkv_ref) | copy-start | bytes 4718596
  41.0 6.0 %collective-permute-start.6 = (bf16[4,128,128]{2,1,0:T(8,128)(2,1)}, bf16[4,128,128]{2,1,0:T(8,128)(2,1)}, u32[]{:S(2)}, u32[]{:S(2)}) collective-permute-start(bf16[4,128,128]{2,1,0:T(8,128)(2,1)} %dynamic-slice_convert_fusion.1), channel_id=1, source_target_pairs={{0,4},{4,0},{8,12},{12,8},{16,20},{20,16},{24,28},{28,24},{32,36},... | collective-permute-start | bytes 393224 | tf_op jit(solution)/shard_map/ppermute | solution.py:385
  43.1 37.2 %collective-permute-start.10 = (bf16[256,768]{1,0:T(8,128)(2,1)S(1)}, bf16[256,768]{1,0:T(8,128)(2,1)S(1)}, u32[]{:S(2)}, u32[]{:S(2)}) collective-permute-start(bf16[256,768]{1,0:T(8,128)(2,1)S(1)} %copy-done.7), channel_id=1, source_target_pairs={{0,3},{1,0},{2,1},{3,2},{4,7},{5,4},{6,5},{7,6},{8,11},{9,8},{10,9... | collective-permute-start | bytes 1179656 | tf_op jit(solution)/shard_map/ppermute | solution.py:372
  44.7 35.6 %collective-permute-start.8 = (bf16[256,768]{1,0:T(8,128)(2,1)S(1)}, bf16[256,768]{1,0:T(8,128)(2,1)S(1)}, u32[]{:S(2)}, u32[]{:S(2)}) collective-permute-start(bf16[256,768]{1,0:T(8,128)(2,1)S(1)} %copy-done.7), channel_id=1, source_target_pairs={{0,2},{1,3},{2,0},{3,1},{4,6},{5,7},{6,4},{7,5},{8,10},{9,11},{10,... | collective-permute-start | bytes 1179656 | tf_op jit(solution)/shard_map/ppermute | solution.py:372
  46.1 34.2 %collective-permute-start.9 = (bf16[256,768]{1,0:T(8,128)(2,1)S(1)}, bf16[256,768]{1,0:T(8,128)(2,1)}, u32[]{:S(2)}, u32[]{:S(2)}) collective-permute-start(bf16[256,768]{1,0:T(8,128)(2,1)S(1)} %copy-done.7), channel_id=1, source_target_pairs={{0,1},{1,2},{2,3},{3,0},{4,5},{5,6},{6,7},{7,4},{8,9},{9,10},{10,1... | collective-permute-start | bytes 1179656 | tf_op jit(solution)/shard_map/ppermute | solution.py:372
  48.5 14.5 %all-to-all-start = ((bf16[16,32,128]{2,1,0:T(8,128)(2,1)}), bf16[16,32,128]{2,1,0:T(8,128)(2,1)}, u32[]{:S(2)}, u32[]{:S(2)}) async-start(bf16[16,32,128]{2,1,0:T(8,128)(2,1)} %bitcast.169), calls=%async_computation | async-start | bytes 262144 | tf_op jit(solution)/shard_map/all_to_all | solution.py:400
  64.8 11.1 %all-to-all-start.1 = ((bf16[16,32,128]{2,1,0:T(8,128)(2,1)}), bf16[16,32,128]{2,1,0:T(8,128)(2,1)}, u32[]{:S(2)}, u32[]{:S(2)}) async-start(bf16[16,32,128]{2,1,0:T(8,128)(2,1)} %fusion.2), calls=%async_computation.1 | async-start | bytes 262144 | tf_op jit(solution)/shard_map/all_to_all | solution.py:403
  76.8 11.6 %collective-permute-start.7 = (bf16[4,128,128]{2,1,0:T(8,128)(2,1)S(1)}, bf16[4,128,128]{2,1,0:T(8,128)(2,1)S(1)}, u32[]{:S(2)}, u32[]{:S(2)}) collective-permute-start(bf16[4,128,128]{2,1,0:T(8,128)(2,1)S(1)} %fusion.7), channel_id=1, source_target_pairs={{0,4},{4,0},{8,12},{12,8},{16,20},{20,16},{24,28},{28,24},{32,36},... | collective-permute-start | bytes 393224 | tf_op jit(solution)/shard_map/ppermute | solution.py:385
  88.4 19.9 %copy-start.22 = (bf16[16,1024]{1,0:T(8,128)(2,1)S(1)}, bf16[16,1024]{1,0:T(8,128)(2,1)}, u32[]{:S(2)}) copy-start(bf16[16,1024]{1,0:T(8,128)(2,1)} %slice_bitcast_fusion.12.up_ref) | copy-start | bytes 98308
  96.6 11.7 %copy-start.17 = (bf16[256,1024]{1,0:T(8,128)(2,1)}, bf16[256,1024]{1,0:T(8,128)(2,1)S(1)}, u32[]{:S(2)}) copy-start(bf16[256,1024]{1,0:T(8,128)(2,1)S(1)} %get-tuple-element.23.att_ref) | copy-start | bytes 1572868
  97.7 4.7 %collective-permute-start.14 = (bf16[4,128,128]{2,1,0:T(8,128)(2,1)S(1)}, bf16[4,128,128]{2,1,0:T(8,128)(2,1)S(1)}, u32[]{:S(2)}, u32[]{:S(2)}) collective-permute-start(bf16[4,128,128]{2,1,0:T(8,128)(2,1)S(1)} %dynamic-slice_convert_fusion), channel_id=1, source_target_pairs={{0,4},{4,0},{8,12},{12,8},{16,20},{20,16},{24,28},{28,24},{32,36},... | collective-permute-start | bytes 393224 | tf_op jit(solution)/shard_map/ppermute | solution.py:385
  98.5 26.0 %collective-permute-start.11 = (bf16[256,16]{1,0:T(8,128)(2,1)}, bf16[256,16]{1,0:T(8,128)(2,1)}, u32[]{:S(2)}, u32[]{:S(2)}) collective-permute-start(bf16[256,16]{1,0:T(8,128)(2,1)} %convert_element_type.143), channel_id=1, source_target_pairs={{0,2},{1,3},{2,0},{3,1},{4,6},{5,7},{6,4},{7,5},{8,10},{9,11},{10,... | collective-permute-start | bytes 24584 | tf_op jit(solution)/shard_map/ppermute | solution.py:372
  99.8 24.8 %collective-permute-start.12 = (bf16[256,16]{1,0:T(8,128)(2,1)}, bf16[256,16]{1,0:T(8,128)(2,1)}, u32[]{:S(2)}, u32[]{:S(2)}) collective-permute-start(bf16[256,16]{1,0:T(8,128)(2,1)} %convert_element_type.143), channel_id=1, source_target_pairs={{0,1},{1,2},{2,3},{3,0},{4,5},{5,6},{6,7},{7,4},{8,9},{9,10},{10,1... | collective-permute-start | bytes 24584 | tf_op jit(solution)/shard_map/ppermute | solution.py:372
  100.7 23.9 %collective-permute-start.13 = (bf16[256,16]{1,0:T(8,128)(2,1)}, bf16[256,16]{1,0:T(8,128)(2,1)}, u32[]{:S(2)}, u32[]{:S(2)}) collective-permute-start(bf16[256,16]{1,0:T(8,128)(2,1)} %convert_element_type.143), channel_id=1, source_target_pairs={{0,3},{1,0},{2,1},{3,2},{4,7},{5,4},{6,5},{7,6},{8,11},{9,8},{10,9... | collective-permute-start | bytes 24584 | tf_op jit(solution)/shard_map/ppermute | solution.py:372
  102.5 5.9 %copy-start.27 = (bf16[4,128,128]{2,1,0:T(8,128)(2,1)}, bf16[4,128,128]{2,1,0:T(8,128)(2,1)S(1)}, u32[]{:S(2)}) copy-start(bf16[4,128,128]{2,1,0:T(8,128)(2,1)S(1)} %collective-permute-done.14) | copy-start | bytes 393220
  104.1 12.1 %all-to-all-start.3 = ((bf16[16,32,128]{2,1,0:T(8,128)(2,1)}), bf16[16,32,128]{2,1,0:T(8,128)(2,1)}, u32[]{:S(2)}, u32[]{:S(2)}) async-start(bf16[16,32,128]{2,1,0:T(8,128)(2,1)} %bitcast.16), calls=%async_computation.3 | async-start | bytes 262144 | tf_op jit(solution)/shard_map/all_to_all | solution.py:400
  116.2 21.4 %copy-start.13 = (f32[256,1024]{1,0:T(8,128)S(1)}, f32[256,1024]{1,0:T(8,128)}, u32[]{:S(2)}) copy-start(f32[256,1024]{1,0:T(8,128)} %copy-done.12) | copy-start | bytes 3145732
  118.0 13.4 %all-to-all-start.4 = ((bf16[16,32,128]{2,1,0:T(8,128)(2,1)}), bf16[16,32,128]{2,1,0:T(8,128)(2,1)S(1)}, u32[]{:S(2)}, u32[]{:S(2)}) async-start(bf16[16,32,128]{2,1,0:T(8,128)(2,1)} %subtract_convert_fusion), calls=%async_computation.4 | async-start | bytes 262144 | tf_op jit(solution)/shard_map/all_to_all | solution.py:403
  125.5 12.1 %copy-start.25 = (bf16[256,16]{1,0:T(8,128)(2,1)}, bf16[256,16]{1,0:T(8,128)(2,1)S(1)}, u32[]{:S(2)}) copy-start(bf16[256,16]{1,0:T(8,128)(2,1)S(1)} %add_convert_fusion.1) | copy-start | bytes 24580
  131.4 6.3 %copy-start.11 = (bf16[3,256,1024]{2,1,0:T(8,128)(2,1)S(1)}, bf16[3,256,1024]{2,1,0:T(8,128)(2,1)}, u32[]{:S(2)}) copy-start(bf16[3,256,1024]{2,1,0:T(8,128)(2,1)} %copy-done.10) | copy-start | bytes 4718596
  132.5 4.1 %collective-permute-start.15 = (bf16[4,128,128]{2,1,0:T(8,128)(2,1)S(1)}, bf16[4,128,128]{2,1,0:T(8,128)(2,1)S(1)}, u32[]{:S(2)}, u32[]{:S(2)}) collective-permute-start(bf16[4,128,128]{2,1,0:T(8,128)(2,1)S(1)} %fusion.9), channel_id=1, source_target_pairs={{0,4},{4,0},{8,12},{12,8},{16,20},{20,16},{24,28},{28,24},{32,36},... | collective-permute-start | bytes 393224 | tf_op jit(solution)/shard_map/ppermute | solution.py:385
  141.8 18.4 %collective-permute-start.16 = (bf16[256,48]{0,1:T(8,128)(2,1)S(1)}, bf16[256,48]{0,1:T(8,128)(2,1)S(1)}, u32[]{:S(2)}, u32[]{:S(2)}) collective-permute-start(bf16[256,48]{0,1:T(8,128)(2,1)S(1)} %fusion.14), channel_id=1, source_target_pairs={{0,2},{1,3},{2,0},{3,1},{4,6},{5,7},{6,4},{7,5},{8,10},{9,11},{10,... | collective-permute-start | bytes 73736 | tf_op jit(solution)/shard_map/ppermute | solution.py:372
  142.3 20.5 %collective-permute-start.17 = (bf16[256,48]{0,1:T(8,128)(2,1)S(1)}, bf16[256,48]{0,1:T(8,128)(2,1)S(1)}, u32[]{:S(2)}, u32[]{:S(2)}) collective-permute-start(bf16[256,48]{0,1:T(8,128)(2,1)S(1)} %fusion.14), channel_id=1, source_target_pairs={{0,1},{1,2},{2,3},{3,0},{4,5},{5,6},{6,7},{7,4},{8,9},{9,10},{10,1... | collective-permute-start | bytes 73736 | tf_op jit(solution)/shard_map/ppermute | solution.py:372
  142.8 20.1 %collective-permute-start.18 = (bf16[256,48]{0,1:T(8,128)(2,1)S(1)}, bf16[256,48]{0,1:T(8,128)(2,1)S(1)}, u32[]{:S(2)}, u32[]{:S(2)}) collective-permute-start(bf16[256,48]{0,1:T(8,128)(2,1)S(1)} %fusion.14), channel_id=1, source_target_pairs={{0,3},{1,0},{2,1},{3,2},{4,7},{5,4},{6,5},{7,6},{8,11},{9,8},{10,9... | collective-permute-start | bytes 73736 | tf_op jit(solution)/shard_map/ppermute | solution.py:372
  145.0 6.4 %copy-start.3 = (bf16[3,3072,1024]{2,1,0:T(8,128)(2,1)S(1)}, bf16[3,3072,1024]{2,1,0:T(8,128)(2,1)}, u32[]{:S(2)}) copy-start(bf16[3,3072,1024]{2,1,0:T(8,128)(2,1)} %weight_ref.11) | copy-start | bytes 56623108
  153.6 51.7 %collective-permute-start.19 = (bf16[256,768]{1,0:T(8,128)(2,1)S(1)}, bf16[256,768]{1,0:T(8,128)(2,1)}, u32[]{:S(2)}, u32[]{:S(2)}) collective-permute-start(bf16[256,768]{1,0:T(8,128)(2,1)S(1)} %shard_map.136), channel_id=1, source_target_pairs={{0,2},{1,3},{2,0},{3,1},{4,6},{5,7},{6,4},{7,5},{8,10},{9,11},{10,... | collective-permute-start | bytes 1179656 | tf_op jit(solution)/shard_map/ppermute | solution.py:372
  157.2 48.2 %collective-permute-start.20 = (bf16[256,768]{1,0:T(8,128)(2,1)S(1)}, bf16[256,768]{1,0:T(8,128)(2,1)}, u32[]{:S(2)}, u32[]{:S(2)}) collective-permute-start(bf16[256,768]{1,0:T(8,128)(2,1)S(1)} %shard_map.137), channel_id=1, source_target_pairs={{0,1},{1,2},{2,3},{3,0},{4,5},{5,6},{6,7},{7,4},{8,9},{9,10},{10,1... | collective-permute-start | bytes 1179656 | tf_op jit(solution)/shard_map/ppermute | solution.py:372
  157.3 5.6 %copy-start.9 = (bf16[256,768]{1,0:T(8,128)(2,1)S(1)}, bf16[256,768]{1,0:T(8,128)(2,1)}, u32[]{:S(2)}) copy-start(bf16[256,768]{1,0:T(8,128)(2,1)} %refs_0_.2) | copy-start | bytes 1179652
  157.3 5.8 %copy-start.29 = (bf16[2,6,8,128]{3,2,1,0:T(8,128)(2,1)S(1)}, bf16[2,6,8,128]{3,2,1,0:T(8,128)(2,1)}, u32[]{:S(2)}) copy-start(bf16[2,6,8,128]{3,2,1,0:T(8,128)(2,1)} %fusion.3) | copy-start | bytes 73732
  157.3 5.9 %copy-start.20 = (f32[8,16,128]{2,1,0:T(8,128)S(1)}, f32[8,16,128]{2,1,0:T(8,128)}, u32[]{:S(2)}) copy-start(f32[8,16,128]{2,1,0:T(8,128)} %copy-done.19) | copy-start | bytes 196612
  157.3 12.2 %copy-start.18 = (bf16[256,1024]{1,0:T(8,128)(2,1)S(1)}, bf16[256,1024]{1,0:T(8,128)(2,1)}, u32[]{:S(2)}) copy-start(bf16[256,1024]{1,0:T(8,128)(2,1)} %copy-done.17) | copy-start | bytes 1572868
  160.2 45.2 %collective-permute-start.21 = (bf16[256,768]{1,0:T(8,128)(2,1)}, bf16[256,768]{1,0:T(8,128)(2,1)}, u32[]{:S(2)}, u32[]{:S(2)}) collective-permute-start(bf16[256,768]{1,0:T(8,128)(2,1)} %shard_map.138), channel_id=1, source_target_pairs={{0,3},{1,0},{2,1},{3,2},{4,7},{5,4},{6,5},{7,6},{8,11},{9,8},{10,9... | collective-permute-start | bytes 1179656 | tf_op jit(solution)/shard_map/ppermute | solution.py:372
  164.0 20.6 %all-to-all-start.5 = ((bf16[32,28,128]{2,1,0:T(8,128)(2,1)}), bf16[32,28,128]{2,1,0:T(8,128)(2,1)S(1)}, u32[]{:S(2)}, u32[]{:S(2)}) async-start(bf16[32,28,128]{2,1,0:T(8,128)(2,1)} %convert_element_type.167), calls=%async_computation.5 | async-start | bytes 524288 | tf_op jit(solution)/shard_map/all_to_all | solution.py:416
  176.0 6.4 %copy-start.4 = (bf16[3,3072,1024]{2,1,0:T(8,128)(2,1)S(1)}, bf16[3,3072,1024]{2,1,0:T(8,128)(2,1)}, u32[]{:S(2)}) copy-start(bf16[3,3072,1024]{2,1,0:T(8,128)(2,1)} %weight_ref.11) | copy-start | bytes 56623108
  185.4 16.4 %all-to-all-start.6 = ((bf16[32,28,128]{2,1,0:T(8,128)(2,1)}), bf16[32,28,128]{2,1,0:T(8,128)(2,1)S(1)}, u32[]{:S(2)}, u32[]{:S(2)}) async-start(bf16[32,28,128]{2,1,0:T(8,128)(2,1)} %broadcast_in_dim.2), calls=%async_computation.6 | async-start | bytes 524288 | tf_op jit(solution)/shard_map/all_to_all | solution.py:419
  201.8 24.2 %all-to-all-start.2 = ((bf16[4,256,768]{2,1,0:T(8,128)(2,1)}), bf16[4,256,768]{2,1,0:T(8,128)(2,1)S(1)}, u32[]{:S(2)}, u32[]{:S(2)}) async-start(bf16[4,256,768]{2,1,0:T(8,128)(2,1)} %shard_map.132), calls=%async_computation.2 | async-start | bytes 3145728 | tf_op jit(solution)/shard_map/all_to_all | solution.py:483
  208.0 18.2 %copy-start.26 = (bf16[256,16]{1,0:T(8,128)(2,1)S(1)}, bf16[256,16]{1,0:T(8,128)(2,1)}, u32[]{:S(2)}) copy-start(bf16[256,16]{1,0:T(8,128)(2,1)} %copy-done.25) | copy-start | bytes 24580
  208.0 18.2 %copy-start.30 = (bf16[16,768]{1,0:T(8,128)(2,1)S(1)}, bf16[16,768]{1,0:T(8,128)(2,1)}, u32[]{:S(2)}) copy-start(bf16[16,768]{1,0:T(8,128)(2,1)} %param.14) | copy-start | bytes 73732
  (12 other events, 17.4 us)
